TPU v7x, 32 devices: a whole 2x2x4 slice. The times are simulated.
32 devices in a mesh: row: 4 (over z), col: 8 (over y, x, core).
Axes of the slice: x: 2, y: 2, z: 4, core: 2. Of those that a mesh axis runs over, the one named last changes fastest.
Arguments:
- amplitudes: bfloat16 [192, 640000], P('col', 'row'), may hold values from -6 to 6
- integrals: bfloat16 [640000, 1600], P(('row', 'col')), may hold values from -0.0078125 to 0.0078125
- occ_irrep: int32 [120], replicated, may hold values from 0 to 7, as said below
- vir_irrep: int32 [800], replicated, may hold values from 0 to 7, as said below
- tile_owner: int32 [96], replicated, may hold values from 0 to 31, as said below
Outputs:
- inbox: bfloat16 [384, 1600], P(('row', 'col'))
Inputs may be any that keep to these rules, and one draw needn't show every extreme that they name: `tile_owner`: no device owns more than 6 tiles and some device owns exactly 6; in every draw the 3 tiles of some device's rows of result all have one owner. `occ_irrep`: labels never decrease along the orbitals, so each irrep's orbitals form one contiguous block. Each of irreps 1 to 7 holds at least one and at most 2 orbitals, one of them exactly that most; irrep 0 holds all the others. `vir_irrep`: labels never decrease along the orbitals, so each irrep's orbitals form one contiguous block. Each of irreps 1 to 7 holds at least one and at most 13 orbitals, one of them exactly that most; irrep 0 holds all the others.
All inputs are finite; a program needn't handle non-finite values.
Results may differ from a plain program's by a relative error of at most 0.0014.
Values may be sent and summed in bfloat16 or wider, within the bound.
A program may use at most 192 MiB of HBM per device.

v0:
```python
import jax
import jax.numpy as jnp
from jax import lax
from jax.sharding import PartitionSpec as P

TR = 2
TILES_DEV = 3
CAP = 6


def lookup(table, index):
    entries = table.shape[0]
    hits = index[:, None] == jnp.arange(entries, dtype=jnp.int32)[None, :]
    return jnp.sum(jnp.where(hits, table[None, :], 0), axis=1)


def on_device(amplitudes, integrals, occ_irrep, vir_irrep, tile_owner):
    ncols = lax.axis_size("col")
    nrows = lax.axis_size("row")
    devices = nrows * ncols
    myself = lax.axis_index("row") * ncols + lax.axis_index("col")
    cd_dev = integrals.shape[0]
    ab_width = integrals.shape[1]
    local_pairs = amplitudes.shape[0]
    pair_count = local_pairs * ncols
    norb = occ_irrep.shape[0]
    nvirt = vir_irrep.shape[0]
    pair_index = jnp.arange(pair_count, dtype=jnp.int32)
    pair_irrep = jnp.bitwise_xor(
        lookup(occ_irrep, pair_index // norb), lookup(occ_irrep, pair_index % norb)
    )
    ab_index = jnp.arange(ab_width, dtype=jnp.int32)
    ab_irrep = jnp.bitwise_xor(
        lookup(vir_irrep, ab_index // nvirt), lookup(vir_irrep, ab_index % nvirt)
    )
    zero_half = jnp.zeros((), jnp.bfloat16)
    panel = lax.all_to_all(amplitudes, "col", split_axis=1, concat_axis=0, tiled=True)
    width = panel.shape[1]
    cd_index = myself * cd_dev + jnp.arange(width, dtype=jnp.int32)
    cd_irrep = jnp.bitwise_xor(
        lookup(vir_irrep, cd_index // nvirt), lookup(vir_irrep, cd_index % nvirt)
    )
    masked_t = jnp.where(pair_irrep[:, None] == cd_irrep[None, :], panel, zero_half)
    masked_v = jnp.where(cd_irrep[:, None] == ab_irrep[None, :], integrals, zero_half)
    ntiles = tile_owner.shape[0]
    tile_ids = jnp.arange(ntiles, dtype=jnp.int32)
    same = tile_owner[:, None] == tile_owner[None, :]
    earlier = tile_ids[:, None] > tile_ids[None, :]
    rank = jnp.sum(jnp.where(same & earlier, 1, 0), axis=1).astype(jnp.int32)
    slot = tile_owner * CAP + rank
    masked_t, masked_v = (masked_t, masked_v)
    total = jnp.dot(masked_t, masked_v, preferred_element_type=jnp.float32)
    summed = lax.psum_scatter(total, ("row", "col"), scatter_dimension=0, tiled=True).astype(
        jnp.bfloat16
    )
    my_tiles = summed.reshape(TILES_DEV, TR * ab_width)
    my_ids = myself * TILES_DEV + jnp.arange(TILES_DEV, dtype=jnp.int32)
    my_owner = lookup(tile_owner, my_ids)
    target = my_owner[None, :] == jnp.arange(devices, dtype=jnp.int32)[:, None]
    outgoing = jnp.where(target[:, :, None], my_tiles[None, :, :], zero_half)
    arrived = lax.all_to_all(outgoing, ("row", "col"), split_axis=0, concat_axis=0, tiled=True)
    picker = (slot[None, :] == myself * CAP + jnp.arange(CAP, dtype=jnp.int32)[:, None]).astype(
        jnp.bfloat16
    )
    placed = jnp.dot(
        picker, arrived.reshape(ntiles, TR * ab_width), preferred_element_type=jnp.float32
    )
    return placed.astype(jnp.bfloat16).reshape(CAP * TR, ab_width)


def solution(mesh):
    in_specs = (P("col", "row"), P(("row", "col"), None), P(), P(), P())
    out_specs = P(("row", "col"), None)
    return jax.shard_map(
        on_device, mesh=mesh, in_specs=in_specs, out_specs=out_specs, check_vma=False
    )
```

profile of v0, /device:TPU:1, one launch (start us, length us, event | category | flops | bytes accessed | tf_op | source)
XLA Modules:
  0.0 227.2 jit_solution(17548316766178148760)
XLA Ops:
  0.0 16.8 %all_to_all.17 = bf16[24,8,20000]{2,1,0:T(8,128)(2,1)} reshape(bf16[24,160000]{1,0:T(8,128)(2,1)} %param.5) | data formatting | bytes 15360000 | tf_op jit(solution)/shard_map/all_to_all | solution.py:37
  16.8 7.0 %copy.8 = bf16[24,8,20000]{2,0,1:T(8,128)(2,1)} copy(bf16[24,8,20000]{2,1,0:T(8,128)(2,1)} %all_to_all.17) | data formatting | bytes 15360000 | tf_op jit(solution)/shard_map/all_to_all | solution.py:37
  23.8 0.0 copy-start
  23.8 0.0 copy-start.1
  23.8 5.4 %all-to-all-start = ((bf16[24,8,20000]{2,0,1:T(8,128)(2,1)}), bf16[24,8,20000]{2,0,1:T(8,128)(2,1)}, u32[]{:S(2)}, u32[]{:S(2)}) async-start(bf16[24,8,20000]{2,0,1:T(8,128)(2,1)} %copy.8), calls=%async_computation | async-start | bytes 15433728 | tf_op jit(solution)/shard_map/all_to_all | solution.py:37
  29.1 0.1 add_select_fusion
  29.2 0.0 copy-done
  29.2 22.1 %select_reduce_fusion = (s32[20000]{0:T(1024)S(1)}, s32[20000]{0:T(1024)S(1)}) fusion(s32[20000]{0:T(1024)S(1)} %get-tuple-element.11, s32[800]{0:T(1024)S(1)} %copy-done, s32[20000]{0:T(1024)S(1)} %get-tuple-element.12), kind=kLoop, calls=%fused_computation.3 | loop fusion | flops 95960000 | bytes 323200 | tf_op jit(solution)/shard_map/reduce_sum | solution.py:14
  51.3 1.9 select_reduce_fusion.2
  53.3 0.0 copy-done.1
  53.3 0.2 select_reduce_fusion.4
  53.6 0.0 copy-done.2
  53.6 0.2 select_reduce_fusion.7
  53.8 58.7 %all-to-all-done = bf16[24,8,20000]{2,0,1:T(8,128)(2,1)} async-done(((bf16[24,8,20000]{2,0,1:T(8,128)(2,1)}), bf16[24,8,20000]{2,0,1:T(8,128)(2,1)}, u32[]{:S(2)}, u32[]{:S(2)}) %all-to-all-start) | async-done | bytes 7680032 | tf_op jit(solution)/shard_map/all_to_all | solution.py:37
  112.5 30.5 %fusion = f32[192,1600]{1,0:T(8,128)S(1)} fusion(bf16[20000,1600]{0,1:T(8,128)(2,1)} %param.6, s32[20000]{0:T(1024)S(1)} %xor.26, s32[1600]{0:T(1024)S(1)} %xor.27, bf16[192,20000]{1,0:T(8,128)(2,1)} %bitcast.1, s32[192]{0:T(256)S(1)} %xor.25), kind=kOutput, calls=%fused_computation.1 | convolution fusion | flops 12359680000 | bytes 72995968 | tf_op jit(solution)/shard_map/dot_general | solution.py:52
  143.0 55.3 %all-reduce.2 = bf16[192,1600]{1,0:T(8,128)(2,1)S(1)} all-reduce(f32[192,1600]{1,0:T(8,128)S(1)} %fusion), channel_id=2, replica_groups=mesh['row'=4,'col'=8] {'row','col'}, use_global_device_ids=true, to_apply=%region_8.9.clone | all-reduce | flops 307200 | bytes 1843200
  198.4 0.1 broadcast_in_dim.145
  198.5 1.2 broadcast_select_fusion
  199.8 5.1 %all-to-all-start.1 = ((bf16[32,3,3200]{2,1,0:T(4,128)(2,1)}), bf16[32,3,3200]{2,1,0:T(4,128)(2,1)S(1)}, u32[]{:S(2)}, u32[]{:S(2)}) async-start(bf16[32,3,3200]{2,1,0:T(4,128)(2,1)} %broadcast_select_fusion), calls=%async_computation.1 | async-start | bytes 1638400 | tf_op jit(solution)/shard_map/all_to_all | solution.py:61
  204.9 0.2 select_reduce_fusion.6
  205.1 20.5 %all-to-all-done.1 = bf16[32,3,3200]{2,1,0:T(4,128)(2,1)S(1)} async-done(((bf16[32,3,3200]{2,1,0:T(4,128)(2,1)}), bf16[32,3,3200]{2,1,0:T(4,128)(2,1)S(1)}, u32[]{:S(2)}, u32[]{:S(2)}) %all-to-all-start.1) | async-done | bytes 614432 | tf_op jit(solution)/shard_map/all_to_all | solution.py:61
  225.6 0.5 reshape.118
  226.2 0.2 convolution_convert_fusion
  226.4 0.8 reshape.119
  (11 shorter events, 0.1 us)
Async XLA Ops:
  23.8 5.5 %copy-start = (s32[800]{0:T(1024)S(1)}, s32[800]{0:T(1024)}, u32[]{:S(2)}) copy-start(s32[800]{0:T(1024)} %param.8) | copy-start | bytes 9604
  23.8 29.5 %copy-start.1 = (s32[120]{0:T(128)S(1)}, s32[120]{0:T(128)}, u32[]{:S(2)}) copy-start(s32[120]{0:T(128)} %param.7) | copy-start | bytes 1444
  23.8 29.8 %copy-start.2 = (s32[96]{0:T(128)S(1)}, s32[96]{0:T(128)}, u32[]{:S(2)}) copy-start(s32[96]{0:T(128)} %param.9) | copy-start | bytes 1156
  23.8 88.8 %all-to-all-start = ((bf16[24,8,20000]{2,0,1:T(8,128)(2,1)}), bf16[24,8,20000]{2,0,1:T(8,128)(2,1)}, u32[]{:S(2)}, u32[]{:S(2)}) async-start(bf16[24,8,20000]{2,0,1:T(8,128)(2,1)} %copy.8), calls=%async_computation | async-start | bytes 15433728 | tf_op jit(solution)/shard_map/all_to_all | solution.py:37
  199.8 25.9 %all-to-all-start.1 = ((bf16[32,3,3200]{2,1,0:T(4,128)(2,1)}), bf16[32,3,3200]{2,1,0:T(4,128)(2,1)S(1)}, u32[]{:S(2)}, u32[]{:S(2)}) async-start(bf16[32,3,3200]{2,1,0:T(4,128)(2,1)} %broadcast_select_fusion), calls=%async_computation.1 | async-start | bytes 1638400 | tf_op jit(solution)/shard_map/all_to_all | solution.py:61
where the time goes:
time: 228 us; the launch traced here: 227 us
  waiting for transfers between devices  79.3 us (35%)
  blocking collectives  55.3 us (24%)
  matrix products  30.7 us (13%)
  other arithmetic  26 us (11%)
  local copies, waits for them, and re-layouts  25.2 us (11%)
  starting transfers between devices  10.5 us (5%)
    all_to_all x1, waiting for transfers between devices, on_device(): lax.all_to_all(amplitudes, 'col', split_axis=1, concat_axis=0, tiled=True)  58.7 us
    unnamed x1, blocking collectives  55.3 us
    dot_general x1, matrix products, on_device(): total = jnp.dot(masked_t, masked_v, preferred_element_type=jnp.float32)  30.5 us
    reduce_sum x4, other arithmetic, lookup(): return jnp.sum(jnp.where(hits, table[None, :], 0), axis=1)  24.4 us
    all_to_all x2, local copies, waits for them, and re-layouts, on_device(): lax.all_to_all(amplitudes, 'col', split_axis=1, concat_axis=0, tiled=True)  23.8 us
    all_to_all x1, waiting for transfers between devices, on_device(): lax.all_to_all(outgoing, ('row', 'col'), split_axis=0, concat_axis=0, til...  20.5 us
    all_to_all x1, starting transfers between devices, on_device(): lax.all_to_all(amplitudes, 'col', split_axis=1, concat_axis=0, tiled=True)  5.36 us
    all_to_all x1, starting transfers between devices, on_device(): lax.all_to_all(outgoing, ('row', 'col'), split_axis=0, concat_axis=0, til...  5.12 us
  transfers between devices with their start and end apart: 2, of which 2 were waited for; matrix products, arithmetic and copies ran while one was open for 11% of the time, Pallas kernels for 0%

commit v1 on v0

v1 whole, which is shorter than its diff:
```python
import functools

import jax
import jax.numpy as jnp
from jax import lax
from jax.experimental import pallas as pl
from jax.experimental.pallas import tpu as pltpu
from jax.sharding import PartitionSpec as P

TR = 2
CAP = 6
LABELS = 8
LANES = 128
AHEAD = 3
MESH = pl.DeviceIdType.MESH
F32 = jnp.float32
BF16 = jnp.bfloat16
I32 = jnp.int32


def cuts(tiles):
    width = max(1, min(20, tiles // 4))
    tail = [max(1, width // 2), max(1, width // 4)]
    rest = tiles - sum(tail)
    count = -(-rest // width)
    sizes = [rest // count + (1 if k < rest % count else 0) for k in range(count)] + tail
    borders = [0]
    for size in sizes:
        borders.append(borders[-1] + size)
    return borders


def label_of(index, firsts):
    total = jnp.zeros(index.shape, I32)
    for first in firsts:
        total = total + jnp.where(index >= first, 1, 0)
    return total


def firsts_of(labels):
    return [
        jnp.sum(jnp.where(labels < g, 1.0, 0.0), axis=1, keepdims=True).astype(I32)
        for g in range(1, LABELS)
    ]


def split_index(start, offset, size, most):
    high = lax.div(start, jnp.int32(size))
    low = start - high * size + offset
    step = jnp.zeros(offset.shape, I32)
    for k in range(1, (size + most) // size + 1):
        step = step + jnp.where(low >= k * size, 1, 0)
    return high + step, low - step * size


def kernel(
    nrow, ncol, width, amp, vt, vedge, occ, vir, owner, out,
    held, masked, slab, acc, part, near, plane, psum, line, lined, whole, ready, plab,
    sent, got, mine, vsem, s1, r1, s2, r2, s3, r3, s4, r4, s5, r5, s6, r6,
):
    local = amp.shape[0]
    abw, cdw = vt.shape
    pairs = local * ncol
    nvirt = vir.shape[1]
    norb = occ.shape[1]
    chips = ncol // 2
    abt = psum.shape[1] // LANES
    zt = line.shape[2] // LANES
    np_ = masked.shape[0]
    mrow = lax.axis_index("row")
    mcol = lax.axis_index("col")
    core = lax.rem(mcol, 2)
    chip = lax.div(mcol, 2)
    me = mrow * ncol + mcol
    borders = cuts(width // LANES)
    count = len(borders) - 1

    def col_of(k):
        return lax.rem(mcol + k, ncol)

    def row_of(k):
        return lax.rem(mrow + k, nrow)

    def chip_of(k):
        return lax.rem(chip + k, chips)

    barrier = pltpu.get_barrier_semaphore()
    for k in range(1, ncol):
        pl.semaphore_signal(barrier, inc=1, device_id=(mrow, col_of(k)), device_id_type=MESH)
    for k in range(1, nrow):
        pl.semaphore_signal(barrier, inc=1, device_id=(row_of(k), mcol), device_id_type=MESH)
    pl.semaphore_wait(barrier, ncol - 1 + nrow - 1)

    def shift_of(col):
        return lax.rem(col * cdw, LANES)

    def span(q):
        low = 0 if q == 0 else (borders[q] + 1) * LANES
        high = min((borders[q + 1] + 1) * LANES, width)
        return low, high - low

    def amp_slice(col, q):
        low, size = span(q)
        start = pl.multiple_of(col * cdw - shift_of(col) + low, LANES)
        return amp.at[:, pl.ds(start, size)]

    def sends(q):
        low, size = span(q)
        return [
            pltpu.make_async_remote_copy(
                src_ref=amp_slice(col_of(k), q),
                dst_ref=held.at[mcol, :, pl.ds(low, size)],
                send_sem=sent.at[q, k - 1],
                recv_sem=got.at[q, k - 1],
                device_id=(mrow, col_of(k)),
                device_id_type=MESH,
            )
            for k in range(1, ncol)
        ]

    def own(q):
        low, size = span(q)
        return pltpu.make_async_copy(
            amp_slice(mcol, q), held.at[mcol, :, pl.ds(low, size)], mine.at[q]
        )

    class Slab:
        def __init__(self, q):
            low = borders[q] * LANES
            size = min(borders[q + 1] * LANES, cdw // LANES * LANES) - low
            self.copies = []
            if size:
                self.copies.append(pltpu.make_async_copy(
                    vt.at[:, pl.ds(low, size)], slab.at[q % 2, :, pl.ds(0, size)], vsem.at[q % 2]
                ))
            if low + size < borders[q + 1] * LANES:
                self.copies.append(pltpu.make_async_copy(
                    vedge, slab.at[q % 2, :, pl.ds(size, LANES)], vsem.at[2]
                ))

        def start(self):
            for copy in self.copies:
                copy.start()

        def wait(self):
            for copy in self.copies:
                copy.wait()

    slab_copy = Slab

    def launch(q):
        for copy in sends(q):
            copy.start()
        own(q).start()

    for q in range(min(AHEAD, count)):
        launch(q)
    slab_copy(0).start()
    if count > 1:
        slab_copy(1).start()

    occ_firsts = firsts_of(occ[...])
    vir_firsts = firsts_of(vir[...])
    row_id = lax.broadcasted_iota(I32, (pairs, LANES), 0)
    first, second = split_index(jnp.int32(0), row_id, norb, pairs)
    plab[...] = jnp.bitwise_xor(label_of(first, occ_firsts), label_of(second, occ_firsts))

    acc[...] = jnp.zeros_like(acc)
    masked[...] = jnp.zeros_like(masked)

    tiles = owner.shape[1]
    is_mine = jnp.where(jnp.broadcast_to(owner[...], (16, tiles)) == me, 1.0, 0.0).astype(BF16)
    tile_id = lax.broadcasted_iota(I32, (tiles, pairs), 0)
    pair_tile = lax.broadcasted_iota(I32, (tiles, pairs), 1) // TR
    spread = jnp.where(tile_id == pair_tile, 1.0, 0.0).astype(BF16)
    before = jnp.where(tile_id < pair_tile, 1.0, 0.0).astype(BF16)
    mine_of = jnp.dot(is_mine, spread, preferred_element_type=F32)
    rank_of = jnp.dot(is_mine, before, preferred_element_type=F32)
    pair_id = lax.broadcasted_iota(I32, (16, pairs), 1)
    place = rank_of.astype(I32) * TR + (pair_id - (pair_id // TR) * TR)
    picker = jnp.where(
        (mine_of > 0.5) & (place == lax.broadcasted_iota(I32, (16, pairs), 0)), 1.0, 0.0
    ).astype(BF16)

    shift = shift_of(mcol)
    turn = lax.rem(LANES - shift, LANES)
    lane = lax.broadcasted_iota(I32, (local, LANES), 1)
    from_here = lane < LANES - shift

    for q in range(count):
        size = borders[q + 1] - borders[q]
        for copy in sends(q):
            copy.wait()
        own(q).wait()
        if q + AHEAD < count:
            launch(q + AHEAD)
        base = me * cdw + borders[q] * LANES
        offset = lax.broadcasted_iota(I32, (1, size * LANES), 1)
        high, low = split_index(base, offset, nvirt, size * LANES)
        cd_label = jnp.bitwise_xor(label_of(high, vir_firsts), label_of(low, vir_firsts))
        inside = offset + borders[q] * LANES < cdw
        cd_label = jnp.where(inside, cd_label, -1)

        def prepare(s, carry, size=size, q=q, cd_label=cd_label):
            halves = []
            for h in range(2):
                src = s * 2 + h
                label = plab[pl.ds(pl.multiple_of(src * local, 8), local), :]
                turned = []
                for j in range(size + 1):
                    tile = borders[q] + j
                    if (tile + 1) * LANES > width:
                        turned.append(turned[-1])
                        continue
                    value = held[src, :, tile * LANES:(tile + 1) * LANES].astype(F32)
                    turned.append(pltpu.roll(value, turn, 1))
                columns = []
                for j in range(size):
                    value = jnp.where(from_here, turned[j], turned[j + 1])
                    keep = cd_label[:, j * LANES:(j + 1) * LANES] == label
                    columns.append(jnp.where(keep, value, 0.0))
                halves.append(columns)
            for j in range(size):
                both = jnp.concatenate([halves[0][j], halves[1][j]], axis=0).astype(BF16)
                start = pl.multiple_of(s * (2 * local), 16)
                masked[pl.ds(start, 2 * local), j * LANES:(j + 1) * LANES] = both
            return carry

        lax.fori_loop(0, chips, prepare, 0)
        slab_copy(q).wait()
        step = 320 if abw % 320 == 0 else abw

        def multiply(m, carry, size=size, q=q, step=step):
            rows = pl.ds(pl.multiple_of(m * step, 16), step)
            acc[rows, :] += lax.dot_general(
                slab[q % 2, rows, 0:size * LANES],
                masked[:, 0:size * LANES],
                (((1,), (1,)), ((), ())),
                preferred_element_type=F32,
            )
            return carry

        lax.fori_loop(0, abw // step, multiply, 0)
        if q + 2 < count:
            slab_copy(q + 2).start()

    for j in range(abt):
        block = acc[j * LANES:(j + 1) * LANES, :].T
        for c in range(ncol):
            part[c % 2, c // 2, :, j * LANES:(j + 1) * LANES] = block[c * local:(c + 1) * local, :]

    other = mrow, chip * 2 + 1 - core
    first_sends = []
    for k in list(range(1, chips)) + [0]:
        copy = pltpu.make_async_remote_copy(
            src_ref=part.at[1 - core, chip_of(k)], dst_ref=near.at[chip_of(k)],
            send_sem=s1.at[k], recv_sem=r1.at[k], device_id=other, device_id_type=MESH,
        )
        copy.start()
        first_sends.append(copy)
    plane_sends = []
    for copy, k in zip(first_sends, list(range(1, chips)) + [0]):
        copy.wait_recv()
        part[core, chip_of(k)] += near[chip_of(k)]
        if k:
            over = pltpu.make_async_remote_copy(
                src_ref=part.at[core, chip_of(k)], dst_ref=plane.at[k - 1],
                send_sem=s2.at[k - 1], recv_sem=r2.at[k - 1],
                device_id=(mrow, chip_of(k) * 2 + core), device_id_type=MESH,
            )
            over.start()
            plane_sends.append(over)
    total = part[core, chip]
    for k, copy in enumerate(plane_sends):
        copy.wait_recv()
        total = total + plane[k]
    psum[...] = total

    def lanes_of(row):
        return pl.multiple_of(jnp.minimum(row * zt, abt - zt) * LANES, LANES)

    row_sends = []
    for k in range(1, nrow):
        copy = pltpu.make_async_remote_copy(
            src_ref=psum.at[:, pl.ds(lanes_of(row_of(k)), zt * LANES)], dst_ref=line.at[k - 1],
            send_sem=s3.at[k - 1], recv_sem=r3.at[k - 1],
            device_id=(row_of(k), mcol), device_id_type=MESH,
        )
        copy.start()
        row_sends.append(copy)
    ab = lanes_of(mrow) + lax.broadcasted_iota(I32, (1, zt * LANES), 1)
    ab_first, ab_second = split_index(jnp.int32(0), ab, nvirt, abt * LANES)
    ab_label = jnp.bitwise_xor(
        label_of(ab_first, vir_firsts), label_of(ab_second, vir_firsts)
    )
    my_label = plab[pl.ds(pl.multiple_of(mcol * local, 8), local), :]
    my_label = jnp.concatenate([my_label] * zt, axis=1)
    summed = psum[:, pl.ds(lanes_of(mrow), zt * LANES)]
    for k, copy in enumerate(row_sends):
        copy.wait_recv()
        summed = summed + line[k]
    lined[mrow] = jnp.where(ab_label == my_label, summed, 0.0).astype(BF16)

    back = []
    for k in range(1, nrow):
        copy = pltpu.make_async_remote_copy(
            src_ref=lined.at[mrow], dst_ref=lined.at[mrow],
            send_sem=s4.at[k - 1], recv_sem=r4.at[k - 1],
            device_id=(row_of(k), mcol), device_id_type=MESH,
        )
        copy.start()
        back.append(copy)
    for copy in back:
        copy.wait_recv()
    for r in range(nrow):
        low = min(r * zt, abt - zt) * LANES
        whole[core, chip, :, low:low + zt * LANES] = lined[r]
    over = []
    for k in range(1, chips):
        copy = pltpu.make_async_remote_copy(
            src_ref=whole.at[core, chip], dst_ref=whole.at[core, chip],
            send_sem=s5.at[k - 1], recv_sem=r5.at[k - 1],
            device_id=(mrow, chip_of(k) * 2 + core), device_id_type=MESH,
        )
        copy.start()
        over.append(copy)
    across = []
    for k in range(chips):
        src = lax.rem(chip - k + chips, chips)
        if k:
            over[k - 1].wait_recv()
        copy = pltpu.make_async_remote_copy(
            src_ref=whole.at[core, src], dst_ref=whole.at[core, src],
            send_sem=s6.at[k], recv_sem=r6.at[k], device_id=other, device_id_type=MESH,
        )
        copy.start()
        across.append(copy)
    for copy in across:
        copy.wait_recv()
    for c in range(chips):
        both = jnp.concatenate([whole[0, c].astype(F32), whole[1, c].astype(F32)], axis=0)
        ready[c * 2 * local:(c + 1) * 2 * local, :] = both.astype(BF16)
    picked = jnp.dot(picker, ready[...], preferred_element_type=F32)
    out[...] = picked[0:CAP * TR, 0:abw].astype(BF16)
    for copy in first_sends + plane_sends + row_sends + back + over + across:
        copy.wait_send()


def on_device(amplitudes, integrals, occ_irrep, vir_irrep, tile_owner):
    ncol = lax.axis_size("col")
    nrow = lax.axis_size("row")
    local, cd_row = amplitudes.shape
    cdw, abw = integrals.shape
    pairs = local * ncol
    chips = ncol // 2
    most = max((c * cdw) % LANES for c in range(ncol))
    width = -(-(cdw + most) // LANES) * LANES
    for c in range(ncol):
        assert c * cdw - (c * cdw) % LANES + width <= cd_row
    borders = cuts(width // LANES)
    count = len(borders) - 1
    widest = max(b - a for a, b in zip(borders, borders[1:])) * LANES
    abt = -(-abw // LANES)
    zt = -(-abt // nrow)
    padded = -(-pairs // LANES) * LANES
    assert width - LANES < cdw < width
    edge = jnp.pad(integrals[width - LANES:, :].T, ((0, 0), (0, width - cdw)))
    vmem = pl.BlockSpec(memory_space=pltpu.VMEM)
    hbm = pl.BlockSpec(memory_space=pl.ANY)

    def dma(*shape):
        return pltpu.SemaphoreType.DMA(shape)

    stages = [chips, chips - 1, nrow - 1, nrow - 1, chips - 1, chips]
    return pl.pallas_call(
        functools.partial(kernel, nrow, ncol, width),
        out_shape=jax.ShapeDtypeStruct((CAP * TR, abw), BF16),
        in_specs=[hbm, hbm, hbm, vmem, vmem, vmem],
        out_specs=vmem,
        scratch_shapes=[
            pltpu.VMEM((ncol, local, width), BF16),
            pltpu.VMEM((padded, widest), BF16),
            pltpu.VMEM((2, abw, widest), BF16),
            pltpu.VMEM((abt * LANES, padded), F32),
            pltpu.VMEM((2, chips, local, abt * LANES), F32),
            pltpu.VMEM((chips, local, abt * LANES), F32),
            pltpu.VMEM((chips - 1, local, abt * LANES), F32),
            pltpu.VMEM((local, abt * LANES), F32),
            pltpu.VMEM((nrow - 1, local, zt * LANES), F32),
            pltpu.VMEM((nrow, local, zt * LANES), BF16),
            pltpu.VMEM((2, chips, local, abt * LANES), BF16),
            pltpu.VMEM((pairs, abt * LANES), BF16),
            pltpu.VMEM((pairs, LANES), I32),
            dma(count, ncol - 1),
            dma(count, ncol - 1),
            dma(count),
            dma(3),
        ]
        + [dma(n) for n in stages for _ in range(2)],
        compiler_params=pltpu.CompilerParams(
            collective_id=0, has_side_effects=True, vmem_limit_bytes=60 * 1024 * 1024
        ),
        cost_estimate=pl.CostEstimate(
            flops=2 * pairs * cdw * abw, bytes_accessed=2 * cdw * abw, transcendentals=0
        ),
    )(
        amplitudes,
        integrals.T,
        edge,
        occ_irrep.reshape(1, -1),
        vir_irrep.reshape(1, -1),
        tile_owner.reshape(1, -1),
    )


def solution(mesh):
    in_specs = (P("col", "row"), P(("row", "col"), None), P(), P(), P())
    out_specs = P(("row", "col"), None)
    return jax.shard_map(
        on_device, mesh=mesh, in_specs=in_specs, out_specs=out_specs, check_vma=False
    )
```

time: 228 us -> 127 us (0.56)
  Pallas kernels: 0 us -> 122 us
  waiting for transfers between devices: 79.3 us -> 0 us
  blocking collectives: 55.3 us -> 0 us
  matrix products: 30.7 us -> 0 us
  other arithmetic: 26 us -> 0 us
  local copies, waits for them, and re-layouts: 25.2 us -> 4.55 us
  starting transfers between devices: 10.5 us -> 0 us
    pallas_call x0 -> x1, Pallas kernels: none -> 122 us  [on_device(): pl.pallas_call(functools.partial(kernel, nrow, ncol, width), out_shape=ja...]
    all_to_all x2 -> x0, waiting for transfers between devices: 79.3 us -> none  [the longest x1 58.7 us: on_device(): lax.all_to_all(amplitudes, 'col', split_axis=1, concat_axis=0, tiled=True)]
    unnamed x1 -> x0, blocking collectives: 55.3 us -> none
    dot_general x2 -> x0, matrix products: 30.7 us -> none  [the longest x1 30.5 us: on_device(): total = jnp.dot(masked_t, masked_v, preferred_element_type=jnp.float32)]
    reduce_sum x5 -> x0, other arithmetic: 24.6 us -> none  [the longest x4 24.4 us: lookup(): return jnp.sum(jnp.where(hits, table[None, :], 0), axis=1)]
    all_to_all x2 -> x0, local copies, waits for them, and re-layouts: 23.8 us -> none  [on_device(): lax.all_to_all(amplitudes, 'col', split_axis=1, concat_axis=0, tiled=True)]
    all_to_all x2 -> x0, starting transfers between devices: 10.5 us -> none  [the longest x1 5.36 us: on_device(): lax.all_to_all(amplitudes, 'col', split_axis=1, concat_axis=0, tiled=True)]
  transfers between devices with their start and end apart: 2 -> 0, of which waited for: 2 -> 0; matrix products, arithmetic and copies ran while one was open for 11% -> 0% of each run, Pallas kernels for 0% -> 0%
where the time goes in v1:
time: 127 us
  Pallas kernels  122 us (96%)
  local copies, waits for them, and re-layouts  4.55 us (4%)
    pallas_call x1, Pallas kernels, on_device(): pl.pallas_call(functools.partial(kernel, nrow, ncol, width), out_shape=ja...  122 us

profile of v1, /device:TPU:1, one launch (start us, length us, event | category | flops | bytes accessed | tf_op | source)
XLA Modules:
  0.0 126.9 jit_solution(15540992169085474485)
XLA Ops:
  0.0 1.0 slice_bitcast_fusion
  1.0 0.8 pad.4.vedge
  1.9 1.3 reshape.10.vir
  3.1 122.3 %shard_map.55 = bf16[12,1600]{1,0:T(8,128)(2,1)} custom-call(bf16[24,160000]{1,0:T(8,128)(2,1)} %amp.1, bf16[1600,20000]{1,0:T(8,128)(2,1)} %bitcast.5, bf16[1600,128]{1,0:T(8,128)(2,1)} %pad.4.vedge, s32[1,120]{1,0:T(1,128)} %bitcast.6, s32[1,800]{1,0:T(1,128)} %reshape.10.vir, s32[1,96]{1,0:T(1,128)} %bitcast.7), custom_call_target="tpu_custom_call" | custom-call | flops 12288000000 | bytes 64000000 | tf_op jit(solution)/shard_map/pallas_call | solution.py:375
  125.4 1.4 %copy.7 = bf16[12,1600]{1,0:T(8,128)(2,1)} copy(bf16[12,1600]{1,0:T(8,128)(2,1)} %shard_map.55) | data formatting | bytes 76800

commit v2 on v1

--- a/solution.py
+++ b/solution.py
@@ -44,6 +44,18 @@
     ]
 
 
+def count_below(labels, g):
+    total = labels.shape[0]
+    low = jnp.int32(0)
+    bit = 1 << (total.bit_length() - 1)
+    while bit:
+        tried = low + bit
+        under = labels[jnp.minimum(tried, total) - 1] < g
+        low = jnp.where(under & (tried <= total), tried, low)
+        bit //= 2
+    return low
+
+
 def split_index(start, offset, size, most):
     high = lax.div(start, jnp.int32(size))
     low = start - high * size + offset
@@ -61,7 +73,7 @@
     local = amp.shape[0]
     abw, cdw = vt.shape
     pairs = local * ncol
-    nvirt = vir.shape[1]
+    nvirt = vir.shape[0]
     norb = occ.shape[1]
     chips = ncol // 2
     abt = psum.shape[1] // LANES
@@ -76,7 +88,15 @@
     count = len(borders) - 1
 
     def col_of(k):
-        return lax.rem(mcol + k, ncol)
+        col = mcol
+        bit = 1
+        while bit < ncol:
+            if (k // bit) % 2:
+                col = col + bit - 2 * bit * lax.rem(lax.div(mcol, bit), 2)
+            bit *= 2
+        return col
+
+    order = list(range(2, ncol, 2)) + list(range(3, ncol, 2)) + [1]
 
     def row_of(k):
         return lax.rem(mrow + k, nrow)
@@ -115,7 +135,7 @@
                 device_id=(mrow, col_of(k)),
                 device_id_type=MESH,
             )
-            for k in range(1, ncol)
+            for k in order
         ]
 
     def own(q):
@@ -133,10 +153,6 @@
                 self.copies.append(pltpu.make_async_copy(
                     vt.at[:, pl.ds(low, size)], slab.at[q % 2, :, pl.ds(0, size)], vsem.at[q % 2]
                 ))
-            if low + size < borders[q + 1] * LANES:
-                self.copies.append(pltpu.make_async_copy(
-                    vedge, slab.at[q % 2, :, pl.ds(size, LANES)], vsem.at[2]
-                ))
 
         def start(self):
             for copy in self.copies:
@@ -160,7 +176,7 @@
         slab_copy(1).start()
 
     occ_firsts = firsts_of(occ[...])
-    vir_firsts = firsts_of(vir[...])
+    vir_firsts = [count_below(vir, g) for g in range(1, LABELS)]
     row_id = lax.broadcasted_iota(I32, (pairs, LANES), 0)
     first, second = split_index(jnp.int32(0), row_id, norb, pairs)
     plab[...] = jnp.bitwise_xor(label_of(first, occ_firsts), label_of(second, occ_firsts))
@@ -228,6 +244,10 @@
 
         lax.fori_loop(0, chips, prepare, 0)
         slab_copy(q).wait()
+        if borders[q + 1] * LANES > cdw:
+            edge = (size - 1) * LANES
+            slab[q % 2, :, edge:edge + LANES] = jnp.zeros((abw, LANES), BF16)
+            slab[q % 2, :, edge:edge + vedge.shape[1]] = vedge[...]
         step = 320 if abw % 320 == 0 else abw
 
         def multiply(m, carry, size=size, q=q, step=step):
@@ -351,6 +371,7 @@
     nrow = lax.axis_size("row")
     local, cd_row = amplitudes.shape
     cdw, abw = integrals.shape
+    assert ncol & (ncol - 1) == 0
     pairs = local * ncol
     chips = ncol // 2
     most = max((c * cdw) % LANES for c in range(ncol))
@@ -364,9 +385,10 @@
     zt = -(-abt // nrow)
     padded = -(-pairs // LANES) * LANES
     assert width - LANES < cdw < width
-    edge = jnp.pad(integrals[width - LANES:, :].T, ((0, 0), (0, width - cdw)))
+    edge = integrals[width - LANES:, :].T
     vmem = pl.BlockSpec(memory_space=pltpu.VMEM)
     hbm = pl.BlockSpec(memory_space=pl.ANY)
+    smem = pl.BlockSpec(memory_space=pltpu.SMEM)
 
     def dma(*shape):
         return pltpu.SemaphoreType.DMA(shape)
@@ -375,7 +397,7 @@
     return pl.pallas_call(
         functools.partial(kernel, nrow, ncol, width),
         out_shape=jax.ShapeDtypeStruct((CAP * TR, abw), BF16),
-        in_specs=[hbm, hbm, hbm, vmem, vmem, vmem],
+        in_specs=[hbm, hbm, vmem, vmem, smem, vmem],
         out_specs=vmem,
         scratch_shapes=[
             pltpu.VMEM((ncol, local, width), BF16),
@@ -394,7 +416,7 @@
             dma(count, ncol - 1),
             dma(count, ncol - 1),
             dma(count),
-            dma(3),
+            dma(2),
         ]
         + [dma(n) for n in stages for _ in range(2)],
         compiler_params=pltpu.CompilerParams(
@@ -408,7 +430,7 @@
         integrals.T,
         edge,
         occ_irrep.reshape(1, -1),
-        vir_irrep.reshape(1, -1),
+        vir_irrep,
         tile_owner.reshape(1, -1),
     )
 

time: 127 us -> 126 us (level)
  local copies, waits for them, and re-layouts: 4.55 us -> 3.2 us
where the time goes in v2:
time: 126 us
  Pallas kernels  122 us (97%)
  local copies, waits for them, and re-layouts  3.2 us (3%)
    pallas_call x1, Pallas kernels, on_device(): pl.pallas_call(functools.partial(kernel, nrow, ncol, width), out_shape=ja...  122 us

profile of v2, /device:TPU:1, one launch (start us, length us, event | category | flops | bytes accessed | tf_op | source)
XLA Modules:
  0.0 125.6 jit_solution(7404103828841988187)
XLA Ops:
  0.0 1.8 %slice_bitcast_fusion.vedge = bf16[1600,32]{1,0:T(8,128)(2,1)} fusion(bf16[20000,1600]{0,1:T(8,128)(2,1)} %param.6), kind=kLoop, calls=%fused_computation | loop fusion | bytes 204800 | tf_op jit(solution)/shard_map/transpose | solution.py:388
  1.8 122.4 %shard_map.55 = bf16[12,1600]{1,0:T(8,128)(2,1)} custom-call(bf16[24,160000]{1,0:T(8,128)(2,1)} %amp.1, bf16[1600,20000]{1,0:T(8,128)(2,1)} %bitcast.5, bf16[1600,32]{1,0:T(8,128)(2,1)} %slice_bitcast_fusion.vedge, s32[1,120]{1,0:T(1,128)} %bitcast.6, s32[800]{0:T(1024)} %vir.1, s32[1,96]{1,0:T(1,128)} %bitcast.7), custom_call_target="tpu_custom_call" | custom-call | flops 12288000000 | bytes 64000000 | tf_op jit(solution)/shard_map/pallas_call | solution.py:397
  124.2 1.4 %copy.7 = bf16[12,1600]{1,0:T(8,128)(2,1)} copy(bf16[12,1600]{1,0:T(8,128)(2,1)} %shard_map.55) | data formatting | bytes 76800
